TPU v7x, 512 devices: a whole 4x8x8 slice. The times are simulated.
512 devices in a mesh: dp: 2 (over x_hi), ffn: 16 (over z, core), hid: 16 (over y, x_lo).
Axes of the slice: x: 4 (x_hi: 2, x_lo: 2; x = x_hi * 2 + x_lo), y: 8, z: 8, core: 2. Of those that a mesh axis runs over, the one named last changes fastest.
Arguments:
- stream: bfloat16 [512, 16384], P('dp', 'hid'), may hold values from -160 to 160
- steering: float32 [16384], P('hid'), may hold values from -40 to 40
- strength: float32 [512], P('dp'), may hold values from 0.5 to 2
- norm_gain_vector: float32 [16384], P('hid'), may hold values from 0.25 to 1.75
- frozen_weights: bfloat16 [2, 16384, 26624], P('dp', 'hid', 'ffn'), may hold values from -0.046875 to 0.046875
- adapter_down_factors: bfloat16 [2, 16384, 16], P(None, 'hid'), may hold values from -0.046875 to 0.046875
- adapter_up_factors: bfloat16 [2, 16, 26624], P(None, None, 'ffn'), may hold values from -1.5 to 1.5
- cotangent: bfloat16 [512, 26624], P(('dp', 'hid'), 'ffn'), may hold values from -6 to 6
Outputs:
- residual_stream_gradient: bfloat16 [512, 16384], P('dp', 'hid')
- steering_vector_gradient: float32 [16384], P('hid')
- adapter_down_gradient: float32 [2, 16384, 16], P(None, 'hid')
- adapter_up_gradient: float32 [2, 16, 26624], P(None, None, 'ffn')
All inputs are finite; a program needn't handle non-finite values.
Results may differ from a plain program's by a relative error of at most 0.0068.
Values may be sent and summed in bfloat16 or wider, within the bound.
A program may use at most 64 MiB of HBM per device.

v0:
```python
import jax
import jax.numpy as jnp
from jax import lax
from jax.sharding import PartitionSpec as P

MODEL_WIDTH = 16384


ADAPTER_SCALE = 0.5


def gated_layer_backward(
    preactivation_values, adapter_input_rows, adapter_up_factors, incoming_gradient
):
    activation_values = preactivation_values + ADAPTER_SCALE * jnp.einsum(
        "dch,chn->dcn", adapter_input_rows, adapter_up_factors, preferred_element_type=jnp.float32
    )
    gate_values = activation_values[:, 0]
    up_projection_values = activation_values[:, 1]
    sigma = jax.nn.sigmoid(gate_values)
    flow = incoming_gradient.astype(jnp.float32)
    gate_grad = flow * up_projection_values * sigma * (1.0 + gate_values * (1.0 - sigma))
    upper_grad = flow * gate_values * sigma
    return jnp.stack([gate_grad, upper_grad], axis=1).astype(jnp.bfloat16)


def local(
    stream,
    steering,
    strength,
    norm_gain_vector,
    frozen_weights,
    adapter_down_factors,
    adapter_up_factors,
    cotangent,
):
    rows = stream.astype(jnp.float32)
    row_squares = jnp.sum(rows * rows, axis=1)
    steer_power = jnp.sum(steering * steering)
    total_rows, total_steer = lax.psum((row_squares, steer_power), "hid")
    stream_ms = total_rows / MODEL_WIDTH + 1e-06
    steer_ms = total_steer / MODEL_WIDTH + 1e-06
    scale = strength * jnp.sqrt(stream_ms / steer_ms)
    steered = rows + scale[:, None] * steering[None, :]
    steered_power = lax.psum(jnp.sum(steered * steered, axis=1), "hid")
    inv_rms = lax.rsqrt(steered_power / MODEL_WIDTH + 1e-05)
    normalized_input = (steered * inv_rms[:, None] * norm_gain_vector[None, :]).astype(jnp.bfloat16)
    down_piece = jnp.einsum(
        "jq,hqp->jhp", normalized_input, adapter_down_factors, preferred_element_type=jnp.float32
    )
    weights = lax.all_gather(frozen_weights, "dp", axis=0, tiled=True)
    full_acts = jnp.einsum(
        "td,kdf->tkf", normalized_input, weights, preferred_element_type=jnp.float32
    )
    preactivation_values, adapter_sum = lax.psum((full_acts, down_piece), "hid")
    incoming_gradient = lax.all_gather(cotangent, "hid", axis=0, tiled=True)
    adapter_input_rows = adapter_sum.astype(jnp.bfloat16)
    activation_gradient = gated_layer_backward(
        preactivation_values, adapter_input_rows, adapter_up_factors, incoming_gradient
    )
    grad_share = lax.psum_scatter(
        jnp.einsum("tkf,kdf->td", activation_gradient, weights, preferred_element_type=jnp.float32),
        "ffn",
        scatter_dimension=0,
        tiled=True,
    )
    input_frozen_term = lax.all_gather(grad_share, "ffn", axis=0, tiled=True)
    backward_piece = jnp.einsum(
        "sua,uqa->suq", activation_gradient, adapter_up_factors, preferred_element_type=jnp.float32
    )
    back_sum = lax.psum(backward_piece, "ffn")
    lowrank_backward = back_sum.astype(jnp.bfloat16)
    normalized_gradient = input_frozen_term + ADAPTER_SCALE * jnp.einsum(
        "qme,mfe->qf", lowrank_backward, adapter_down_factors, preferred_element_type=jnp.float32
    )
    product = (
        lax.psum(jnp.sum(steered * norm_gain_vector[None, :] * normalized_gradient, axis=1), "hid")
        / MODEL_WIDTH
    )
    steered_grad = (
        inv_rms[:, None] * norm_gain_vector[None, :] * normalized_gradient
        - (inv_rms**3 * product)[:, None] * steered
    )
    residual_stream_gradient = steered_grad.astype(jnp.bfloat16)
    steering_part = jnp.sum(scale[:, None] * steered_grad, axis=0)
    down_projection_gradient = ADAPTER_SCALE * jnp.einsum(
        "cl,can->aln", normalized_input, lowrank_backward, preferred_element_type=jnp.float32
    )
    up_projection_gradient = ADAPTER_SCALE * jnp.einsum(
        "qyj,qyi->yji", adapter_input_rows, activation_gradient, preferred_element_type=jnp.float32
    )
    down_projection_gradient, up_projection_gradient, steering_vector_gradient = lax.psum(
        (down_projection_gradient, up_projection_gradient, steering_part), "dp"
    )
    return (
        residual_stream_gradient,
        steering_vector_gradient,
        down_projection_gradient,
        up_projection_gradient,
    )


def solution(mesh):
    in_specs = (
        P("dp", "hid"),
        P("hid"),
        P("dp"),
        P("hid"),
        P("dp", "hid", "ffn"),
        P(None, "hid", None),
        P(None, None, "ffn"),
        P(("dp", "hid"), "ffn"),
    )
    out_specs = (P("dp", "hid"), P("hid"), P(None, "hid", None), P(None, None, "ffn"))
    return jax.shard_map(local, mesh=mesh, in_specs=in_specs, out_specs=out_specs, check_vma=False)
```

profile of v0, /device:TPU:1, one launch (start us, length us, event | category | flops | bytes accessed | tf_op | source)
XLA Modules:
  0.0 484.7 jit_solution(4777915458065586716)
XLA Ops:
  7.2 0.0 copy-start
  7.2 0.0 copy-start.5
  7.2 0.0 copy-start.1
  7.2 0.0 copy-start.8
  7.2 0.0 copy-start.7
  7.2 0.0 all-gather.3.cloned.1.call-start
  7.3 0.7 all-gather.3.cloned.1.call-update
  8.0 0.0 all-reduce.5.cloned.1.call-start
  8.0 0.0 copy-done.5
  8.0 0.6 multiply_reduce_fusion.3
  8.6 0.0 copy-done.1
  8.6 0.2 fusion.8
  8.8 29.3 %all-reduce = (f32[256]{0:T(256)S(1)}, f32[]{:T(128)}) all-reduce(f32[256]{0:T(256)S(1)} %fusion.8, f32[]{:T(128)} %multiply_reduce_fusion.3), channel_id=1, replica_groups=mesh['dp'=2,'ffn'=16,'hid'=16] {'hid'}, use_global_device_ids=true, to_apply=%region_1.0 | all-reduce | flops 257 | bytes 2056 | tf_op jit(solution)/shard_map/psum | solution.py:40
  38.8 0.0 copy-done.8
  38.8 0.3 multiply_reduce_fusion.2
  39.1 25.7 %psum.72 = f32[256]{0:T(256)S(1)} all-reduce(f32[256]{0:T(256)S(1)} %multiply_reduce_fusion.2), channel_id=1, replica_groups=mesh['dp'=2,'ffn'=16,'hid'=16] {'hid'}, use_global_device_ids=true, to_apply=%region_5.0 | all-reduce | flops 256 | bytes 2048 | tf_op jit(solution)/shard_map/psum | solution.py:45
  64.9 0.0 copy-done.7
  64.9 0.3 multiply_convert_fusion
  65.1 47.6 %all-gather.3.cloned.1.call-done = bf16[2,1024,1664]{2,1,0:T(8,128)(2,1)} async-done(((bf16[1,1024,1664]{2,1,0:T(8,128)(2,1)}), bf16[2,1024,1664]{2,1,0:T(8,128)(2,1)}) %all-gather.3.cloned.1.call-update) | async-done | bytes 6815760 | tf_op jit(solution)/shard_map/all_gather | solution.py:51
  112.8 6.7 %fusion.12 = f32[256,2,1664]{2,0,1:T(8,128)} fusion(bf16[2,1024,1664]{2,1,0:T(8,128)(2,1)} %all-gather.3.cloned.1.call-done, bf16[256,1024]{1,0:T(8,128)(2,1)S(1)} %multiply_convert_fusion), kind=kOutput, calls=%fused_computation.31 | convolution fusion | flops 1744830464 | bytes 10747904 | tf_op jit(solution)/shard_map/td,kdf->tkf/dot_general | solution.py:52
  119.5 0.0 copy-start.4
  119.5 0.0 copy-start.6
  119.5 0.0 all-reduce.5.cloned.1.call-update
  119.5 0.0 reduce-scatter.2.cloned.1.call-start
  119.6 0.8 copy-done.4
  120.3 0.2 fusion.22
  120.6 50.2 %psum.74 = bf16[256,2,16]{0,2,1:T(8,128)(2,1)S(1)} all-reduce(f32[256,2,16]{0,2,1:T(8,128)S(1)} %bitcast.55), channel_id=1, replica_groups=mesh['dp'=2,'ffn'=16,'hid'=16] {'hid'}, use_global_device_ids=true, to_apply=%region_7.0 | all-reduce | flops 8192 | bytes 49152 | tf_op jit(solution)/shard_map/psum | solution.py:55
  170.8 0.0 copy-done.6
  170.8 53.1 %all_gather.9 = bf16[256,1664]{1,0:T(8,128)(2,1)S(1)} all-gather(bf16[16,1664]{1,0:T(8,128)(2,1)S(1)} %copy-done.6), channel_id=1, replica_groups=mesh['dp'=2,'ffn'=16,'hid'=16] {'hid'}, dimensions={0}, use_global_device_ids=true | all-gather | bytes 905216 | tf_op jit(solution)/shard_map/all_gather | solution.py:56
  223.9 82.8 %all-reduce.5.cloned.1.call-done = f32[256,2,1664]{2,0,1:T(8,128)} async-done(((f32[256,2,1664]{2,0,1:T(8,128)}), f32[256,2,1664]{2,0,1:T(8,128)}) %all-reduce.5.cloned.1.call-update) | async-done | bytes 3407888 | tf_op jit(solution)/shard_map/psum | solution.py:55
  306.7 0.0 copy-done
  306.7 2.6 bitcast_add_fusion
  309.3 0.9 fusion.10
  310.2 0.0 copy-start.2
  310.2 1.0 copy-done.2
  311.2 5.9 %convolution_bitcast_fusion.1 = f32[256,1024]{1,0:T(8,128)} fusion(bf16[2,1024,1664]{2,1,0:T(8,128)(2,1)} %all-gather.3.cloned.1.call-done, bf16[256,1,1664]{2,0,1:T(8,128)(2,1)S(1)} %get-tuple-element.11, bf16[256,1,1664]{2,0,1:T(8,128)(2,1)S(1)} %get-tuple-element.10), kind=kOutput, calls=%fused_computation.16 | convolution fusion | flops 1745682432 | bytes 9568256 | tf_op jit(solution)/shard_map/tkf,kdf->td/dot_general | solution.py:62
  317.0 0.0 reduce-scatter.2.cloned.1.call-update
  317.1 0.0 copy-start.3
  317.1 0.0 all-gather.5.cloned.1.call-start
  317.1 60.2 %reduce-scatter.2.cloned.1.call-done = f32[16,1024]{1,0:T(8,128)} async-done(((f32[256,1024]{1,0:T(8,128)}), f32[16,1024]{1,0:T(8,128)}) %reduce-scatter.2.cloned.1.call-update) | async-done | bytes 65552 | tf_op jit(solution)/shard_map/reduce_scatter | solution.py:61
  377.3 0.0 all-gather.5.cloned.1.call-update
  377.3 0.0 all-reduce.7.cloned.1.call-start
  377.4 1.7 convolution_bitcast_fusion.2
  379.1 46.5 %psum.75 = bf16[256,2,16]{0,2,1:T(8,128)(2,1)S(1)} all-reduce(f32[256,2,16]{0,2,1:T(8,128)S(1)} %convolution_bitcast_fusion.2), channel_id=1, replica_groups=mesh['dp'=2,'ffn'=16,'hid'=16] {'ffn'}, use_global_device_ids=true, to_apply=%region_9.0 | all-reduce | flops 8192 | bytes 49152 | tf_op jit(solution)/shard_map/psum | solution.py:71
  425.6 0.0 copy-done.3
  425.6 1.1 convolution_multiply_fusion
  426.6 0.9 fusion.7
  427.5 0.0 all-reduce.7.cloned.1.call-update
  427.5 0.0 all-gather.5.cloned.1.call-done
  427.6 1.7 multiply_reduce_fusion.1
  429.3 27.7 %psum.76 = f32[256]{0:T(256)S(1)} all-reduce(f32[256]{0:T(256)S(1)} %get-tuple-element.12), channel_id=1, replica_groups=mesh['dp'=2,'ffn'=16,'hid'=16] {'hid'}, use_global_device_ids=true, to_apply=%region_11.0 | all-reduce | flops 256 | bytes 2048 | tf_op jit(solution)/shard_map/psum | solution.py:77
  457.0 1.2 multiply_reduce_fusion
  458.2 5.9 %psum.77 = f32[1024]{0:T(1024)} all-reduce(f32[1024]{0:T(1024)S(1)} %get-tuple-element.8), channel_id=1, replica_groups=mesh['dp'=2,'ffn'=16,'hid'=16] {'dp'}, use_global_device_ids=true, to_apply=%region_13.0 | all-reduce | flops 1024 | bytes 8192 | tf_op jit(solution)/shard_map/psum | solution.py:92
  464.1 10.9 %all-reduce.7.cloned.1.call-done = (f32[2,1024,16]{1,2,0:T(8,128)}, f32[2,16,1664]{2,1,0:T(8,128)}) async-done(((f32[2,1024,16]{1,2,0:T(8,128)}, f32[2,16,1664]{2,1,0:T(8,128)}), (f32[2,1024,16]{1,2,0:T(8,128)}, f32[2,16,1664]{2,1,0:T(8,128)})) %all-reduce.7.cloned.1.call-update) | async-done | bytes 344080 | tf_op jit(solution)/shard_map/psum | solution.py:92
  475.0 1.6 copy.15
  476.5 1.6 copy.16
  (3 shorter events, 0.0 us)
Async XLA Ops:
  7.2 299.6 %copy-start = (bf16[2,16,1664]{2,1,0:T(8,128)(2,1)S(1)}, bf16[2,16,1664]{2,1,0:T(8,128)(2,1)}, u32[]{:S(2)}) copy-start(bf16[2,16,1664]{2,1,0:T(8,128)(2,1)} %param.14) | copy-start | bytes 319492
  7.2 0.8 copy-start.5
  7.2 1.4 copy-start.1
  7.2 31.6 %copy-start.8 = (f32[256]{0:T(256)S(1)}, f32[256]{0:T(256)}, u32[]{:S(2)}) copy-start(f32[256]{0:T(256)} %param.10) | copy-start | bytes 3076
  7.2 57.6 %copy-start.7 = (f32[1024]{0:T(1024)S(1)}, f32[1024]{0:T(1024)}, u32[]{:S(2)}) copy-start(f32[1024]{0:T(1024)} %param.11) | copy-start | bytes 12292
  7.2 105.6 %all-gather.3.cloned.1.call-start = ((), (), s32[]{:S(2)}) async-start(), calls=%async_computation.1 | async-start | bytes 10223616 | tf_op jit(solution)/shard_map/all_gather | solution.py:51
  8.0 298.8 %all-reduce.5.cloned.1.call-start = ((), (), s32[]{:S(2)}) async-start(), calls=%async_computation.2 | async-start | bytes 6815744 | tf_op jit(solution)/shard_map/psum | solution.py:55
  119.5 0.8 copy-start.4
  119.5 51.3 %copy-start.6 = (bf16[16,1664]{1,0:T(8,128)(2,1)S(1)}, bf16[16,1664]{1,0:T(8,128)(2,1)}, u32[]{:S(2)}) copy-start(bf16[16,1664]{1,0:T(8,128)(2,1)} %param.15) | copy-start | bytes 159748
  119.5 257.8 %reduce-scatter.2.cloned.1.call-start = ((), (), s32[]{:S(2)}) async-start(), calls=%async_computation.3 | async-start | bytes 1114112 | tf_op jit(solution)/shard_map/reduce_scatter | solution.py:61
  310.2 1.0 copy-start.2
  317.1 108.5 %copy-start.3 = (bf16[256,1,1664]{2,0,1:T(8,128)(2,1)S(1)}, bf16[256,1,1664]{2,0,1:T(8,128)(2,1)}, u32[]{:S(2)}) copy-start(bf16[256,1,1664]{2,0,1:T(8,128)(2,1)} %copy-done.2) | copy-start | bytes 2555908
  317.1 110.5 %all-gather.5.cloned.1.call-start = ((), (), s32[]{:S(2)}) async-start(), calls=%async_computation.4 | async-start | bytes 1114112 | tf_op jit(solution)/shard_map/all_gather | solution.py:67
  377.3 97.7 %all-reduce.7.cloned.1.call-start = ((), (), s32[]{:S(2)}) async-start(), calls=%async_computation.5 | async-start | bytes 688128 | tf_op jit(solution)/shard_map/psum | solution.py:92
Sparse Core Ops, SparseCore 0:
  10.1 102.5 all-gather.2
  119.6 187.0 all-reduce.4
  317.2 60.0 reduce-scatter.1
  379.3 43.0 all-gather.4
  427.7 47.2 all-reduce.6
where the time goes:
time: 485 us
  blocking collectives  238 us (49%)
  waiting for transfers between devices  202 us (42%)
  matrix products  20.7 us (4%)
  between operations  14.6 us (3%)
  local copies, waits for them, and re-layouts  4.97 us (1%)
    psum x1, waiting for transfers between devices, local(): preactivation_values, adapter_sum = lax.psum((full_acts, down_piece), 'hid')  82.8 us
    reduce_scatter x1, waiting for transfers between devices, local(): lax.psum_scatter(jnp.einsum('tkf,kdf->td', activation_gradient, weights,...  60.2 us
    all_gather x1, blocking collectives, local(): incoming_gradient = lax.all_gather(cotangent, 'hid', axis=0, tiled=True)  53.1 us
    psum x1, blocking collectives, local(): preactivation_values, adapter_sum = lax.psum((full_acts, down_piece), 'hid')  50.2 us
    all_gather x1, waiting for transfers between devices, local(): weights = lax.all_gather(frozen_weights, 'dp', axis=0, tiled=True)  47.6 us
    psum x1, blocking collectives, local(): back_sum = lax.psum(backward_piece, 'ffn')  46.5 us
    psum x1, blocking collectives, local(): total_rows, total_steer = lax.psum((row_squares, steer_power), 'hid')  29.3 us
    psum x1, blocking collectives, local(): lax.psum(jnp.sum(steered * norm_gain_vector[None, :] * normalized_gradien...  27.7 us
  transfers between devices with their start and end apart: 5, of which 4 were waited for; matrix products, arithmetic and copies ran while one was open for 2% of the time, Pallas kernels for 0%

commit v1 on v0

v1 whole, which is shorter than its diff:
```python
import functools

import jax
import jax.numpy as jnp
from jax import lax
from jax.experimental import pallas as pl
from jax.experimental.pallas import tpu as pltpu
from jax.sharding import PartitionSpec as P

ADAPTER_SCALE = 0.5
RANK = 16
ROWS = 16
LANES = 128
MESH = pl.DeviceIdType.MESH
F32 = jnp.float32
BF16 = jnp.bfloat16
NT = (((1,), (1,)), ((), ()))
N_SEMS = 160


def tiles(total, size):
    return [(at, min(size, total - at)) for at in range(0, total, size)]


def row_to_columns(row):
    return jnp.transpose(jnp.broadcast_to(row, (LANES, row.shape[1])))


def columns_to_row(partial):
    return jnp.sum(jnp.transpose(partial), axis=0, keepdims=True)


def kernel(
    model_width, n_hid, n_ffn,
    x_ref, steer_ref, strength_ref, gain_ref, w_hbm, down_ref, up_ref, cot_ref,
    out_ref, steer_grad_ref, down_grad_ref, up_grad_ref,
    w_buf, x_other, stat_a, stat_b, stat_mine, stat_other, steered, cols, normed, partial, y_send, y_recv,
    y_sum, y_block, x_recv, up_ext, down_ext, acts_all, acts_other, back, core_recv, core_sum,
    z_send, z_recv, z_sum, dp_main, dp_ext, gathered, up_mine, up_theirs, steer_mine, steer_theirs,
    send_sem, recv_sem, local_sem,
):
    tokens, width = x_ref.shape
    hidden = w_hbm.shape[1]
    n_y, n_z = n_hid // 2, n_ffn // 2
    dp, fi, hi = lax.axis_index("dp"), lax.axis_index("ffn"), lax.axis_index("hid")
    y, xl, z, core = hi // 2, hi % 2, fi // 2, fi % 2
    first = dp == 0

    to_dp = {"dp": 1 - dp}
    to_xl = {"hid": hi + 1 - 2 * xl}
    to_diag = {"dp": 1 - dp, "hid": hi + 1 - 2 * xl}
    to_core = {"ffn": fi + 1 - 2 * core}
    y_next = ({"hid": lax.rem(hi + 2, n_hid)}, {"hid": lax.rem(hi + n_hid - 2, n_hid)})
    z_next = ({"ffn": lax.rem(fi + 2, n_ffn)}, {"ffn": lax.rem(fi + n_ffn - 2, n_ffn)})

    w_copy = pltpu.make_async_copy(w_hbm, w_buf, local_sem)
    w_copy.start()

    peers = [{"hid": lax.rem(hi + i, n_hid)} for i in range(1, n_hid)]
    peers += [to_dp, to_diag, to_core, *z_next]
    barrier = pltpu.get_barrier_semaphore()
    for peer in peers:
        pl.semaphore_signal(barrier, inc=1, device_id=peer, device_id_type=MESH)
    pl.semaphore_wait(barrier, len(peers))

    started = []

    def send(src, dst, device):
        i = len(started)
        copy = pltpu.make_async_remote_copy(
            src_ref=src, dst_ref=dst, send_sem=send_sem.at[i], recv_sem=recv_sem.at[i],
            device_id=device, device_id_type=MESH,
        )
        copy.start()
        started.append(copy)
        return copy

    half = tokens // 2
    mine = pl.ds(pl.multiple_of(core * half, half), half)
    stream_in = send(x_ref.at[mine], x_other.at[mine], to_dp)

    def sum_over_hid(slots, value):
        slots[hi] = value
        copies = [
            send(slots.at[hi], slots.at[hi], {"hid": lax.rem(hi + i, n_hid)}) for i in range(1, n_hid)
        ]
        for copy in copies:
            copy.wait_recv()
        total = slots[0]
        for i in range(1, n_hid):
            total = total + slots[i]
        return total

    lanes = tiles(width, LANES)
    steer = steer_ref[...]
    gain = gain_ref[...]

    squares = jnp.zeros((tokens, LANES), F32)
    for at, size in lanes:
        piece = x_ref[:, at:at + size].astype(F32)
        squares += piece * piece
    steer_power = jnp.sum(steer * steer, axis=1, keepdims=True)
    sub = lax.broadcasted_iota(jnp.int32, (8, tokens), 0)
    powers = sum_over_hid(
        stat_a,
        jnp.where(
            sub == 0,
            jnp.broadcast_to(columns_to_row(squares), (8, tokens)),
            jnp.broadcast_to(steer_power, (8, tokens)),
        ),
    )
    stream_ms = powers[0:1] / model_width + 1e-06
    steer_ms = powers[1:2] / model_width + 1e-06
    scale = strength_ref[...] * jnp.sqrt(stream_ms / steer_ms)

    scale_cols = row_to_columns(scale)
    cols[0] = scale_cols
    squares = jnp.zeros((tokens, LANES), F32)
    for at, size in lanes:
        piece = x_ref[:, at:at + size].astype(F32) + scale_cols * steer[:, at:at + size]
        steered[:, at:at + size] = piece
        squares += piece * piece
    power = sum_over_hid(stat_b, jnp.broadcast_to(columns_to_row(squares), (8, tokens)))
    inv = lax.rsqrt(power[0:1] / model_width + 1e-05)
    stat_mine[...] = jnp.where(
        sub == 0, jnp.broadcast_to(scale, (8, tokens)), jnp.broadcast_to(inv, (8, tokens))
    )
    stat_in = send(stat_mine, stat_other, to_dp)
    inv_cols = row_to_columns(inv)
    cols[1] = inv_cols
    for at, size in lanes:
        normed[0, :, at:at + size] = (
            steered[:, at:at + size] * inv_cols * gain[:, at:at + size]
        ).astype(BF16)

    up_ext[...] = jnp.zeros(up_ext.shape, BF16)
    up_ext[0:2 * RANK, 0:hidden] = up_ref[...]
    row = lax.broadcasted_iota(jnp.int32, (LANES, LANES), 0)
    col = lax.broadcasted_iota(jnp.int32, (LANES, LANES), 1)
    up_ext[:, hidden:] = jnp.where((row == 32) & ((col == 32) | (col == 33)), 1.0, 0.0).astype(BF16)
    down_ext[...] = jnp.zeros(down_ext.shape, BF16)
    down_ext[0:2 * RANK, :] = down_ref[...]

    w_copy.wait()

    def forward(which):
        rows = normed[which]
        for at, size in tiles(hidden, 256):
            block = jnp.dot(rows, w_buf[:, at:at + size], preferred_element_type=F32)
            partial[which, :, :, at:at + size] = block.reshape(n_y, 2 * ROWS, size)
        block = lax.dot_general(rows, down_ext[...], NT, preferred_element_type=F32)
        partial[which, :, :, hidden:] = block.reshape(n_y, 2 * ROWS, LANES)

    def hops(n, s, d):
        return n // 2 if (s + d) % 2 == 0 else n // 2 - 1

    def reduce_step(n, me, terms, sends, recvs, nexts, flying, s, d, j):
        count = hops(n, s, d)
        if j >= count:
            return
        k = count - j
        owner = lax.rem(me + (k if d == 0 else n - k), n)
        value = terms[s, owner]
        if j:
            flying[s, d, j - 1].wait_recv()
            value = value + recvs[s, d, j - 1].astype(F32)
        sends[s, d, j] = value.astype(BF16)
        flying[s, d, j] = send(sends.at[s, d, j], recvs.at[s, d, j], nexts[d])

    def reduce_end(n, me, terms, recvs, flying, s):
        value = terms[s, me]
        for d in (0, 1):
            count = hops(n, s, d)
            if count:
                flying[s, d, count - 1].wait_recv()
                value = value + recvs[s, d, count - 1].astype(F32)
        return value

    def gather_step(n, me, held, nexts, flying, s, d, j):
        if j >= hops(n, s, d):
            return
        if j:
            flying[s, d, j - 1].wait_recv()
        origin = lax.rem(me + (n - j if d == 0 else j), n)
        flying[s, d, j] = send(held.at[s, origin], held.at[s, origin], nexts[d])

    y_args = (n_y, y, partial, y_send, y_recv, y_next, {})
    forward(0)
    for d in (0, 1):
        reduce_step(*y_args, 0, d, 0)

    stream_in.wait_recv()
    stream_core = send(x_other.at[mine], x_other.at[mine], to_core)
    stat_in.wait_recv()
    stream_core.wait_recv()
    scale_other = row_to_columns(stat_other[0:1])
    inv_other = row_to_columns(stat_other[1:2])
    for at, size in lanes:
        piece = x_other[:, at:at + size].astype(F32) + scale_other * steer[:, at:at + size]
        normed[1, :, at:at + size] = (piece * inv_other * gain[:, at:at + size]).astype(BF16)
    forward(1)
    for d in (0, 1):
        reduce_step(*y_args, 1, d, 0)
    for j in range(1, n_y // 2):
        for s in (0, 1):
            for d in (0, 1):
                reduce_step(*y_args, s, d, j)
    x_in = []
    for s in (0, 1):
        total = reduce_end(n_y, y, partial, y_recv, y_args[-1], s).reshape(2, ROWS, hidden + LANES)
        y_sum[s] = total
        y_block[s] = total.astype(BF16)
        if s == 0:
            x_in.append(send(y_block.at[0, 1 - xl], x_recv.at[0], to_xl))
        else:
            x_in.append(send(y_block.at[1, xl], x_recv.at[1], to_dp))
            x_in.append(send(y_block.at[1, 1 - xl], x_recv.at[2], to_diag))
    for copy in x_in:
        copy.wait_recv()

    acts_same = y_sum[0, xl] + x_recv[0].astype(F32)
    acts_cross = x_recv[1].astype(F32) + x_recv[2].astype(F32)
    gate = jnp.where(first, acts_same, acts_cross)
    up = jnp.where(first, acts_cross, acts_same)
    lane = lax.broadcasted_iota(jnp.int32, (ROWS, LANES), 1)
    low_gate = jnp.where(lane < RANK, gate[:, hidden:], 0.0).astype(BF16)
    low_up = jnp.where((lane >= RANK) & (lane < 2 * RANK), up[:, hidden:], 0.0).astype(BF16)
    factors = up_ext[:, 0:hidden]
    gate = gate[:, 0:hidden] + ADAPTER_SCALE * jnp.dot(low_gate, factors, preferred_element_type=F32)
    up = up[:, 0:hidden] + ADAPTER_SCALE * jnp.dot(low_up, factors, preferred_element_type=F32)
    sigma = 1.0 / (1.0 + jnp.exp(-gate))
    flow = cot_ref[...].astype(F32)
    gate_grad = (flow * up * sigma * (1.0 + gate * (1.0 - sigma))).astype(BF16)
    upper_grad = (flow * gate * sigma).astype(BF16)

    def ext_columns(low, grad, acts):
        inner = jnp.sum(grad.astype(F32) * acts, axis=1, keepdims=True)
        high = inner.astype(BF16).astype(F32)
        rest = jnp.where(lane == 32, high, jnp.where(lane == 33, inner - high, 0.0))
        return low.astype(F32) + rest

    gate_ext = ext_columns(low_gate, gate_grad, gate)
    upper_ext = ext_columns(low_up, upper_grad, up)
    gate_grad, upper_grad = gate_grad.astype(F32), upper_grad.astype(F32)
    acts_all[0, y, xl, :, 0:hidden] = jnp.where(first, gate_grad, upper_grad).astype(BF16)
    acts_all[0, y, xl, :, hidden:] = jnp.where(first, gate_ext, upper_ext).astype(BF16)
    acts_other[:, 0:hidden] = jnp.where(first, upper_grad, gate_grad).astype(BF16)
    acts_other[:, hidden:] = jnp.where(first, upper_ext, gate_ext).astype(BF16)

    x_out = [
        send(acts_all.at[0, y, xl], acts_all.at[0, y, xl], to_xl),
        send(acts_other, acts_all.at[1, y, xl], to_dp),
        send(acts_other, acts_all.at[1, y, xl], to_diag),
    ]
    g_args = (n_y, y, acts_all, y_next, {})
    x_out[0].wait_recv()
    for d in (0, 1):
        gather_step(*g_args, 0, d, 0)
    x_out[1].wait_recv()
    x_out[2].wait_recv()
    for d in (0, 1):
        gather_step(*g_args, 1, d, 0)
    for j in range(1, n_y // 2):
        for s in (0, 1):
            for d in (0, 1):
                gather_step(*g_args, s, d, j)

    wide = lax.broadcasted_iota(jnp.int32, (tokens, LANES), 1)
    keep = ((wide >= RANK * dp) & (wide < RANK * dp + RANK)) | (wide == 32)

    def backward(which):
        for at, size in tiles(width, 256):
            rows = acts_all[which, :, :, :, 0:hidden].reshape(tokens, hidden)
            block = lax.dot_general(rows, w_buf[at:at + size, :], NT, preferred_element_type=F32)
            back[which, :, :, :, at:at + size] = block.reshape(n_z, 2, ROWS, size)
        rows = acts_all[which].reshape(tokens, hidden + LANES)
        block = lax.dot_general(rows, up_ext[...], NT, preferred_element_type=F32)
        back[which, :, :, :, width:] = jnp.where(keep, block, 0.0).reshape(n_z, 2, ROWS, LANES)

    core_in = []
    for s in (0, 1):
        for d in (0, 1):
            count = hops(n_y, s, d)
            if count:
                g_args[-1][s, d, count - 1].wait_recv()
        backward(s)
        core_in.append(send(back.at[s, :, 1 - core], core_recv.at[s], to_core))

    total = jnp.zeros((RANK, hidden), F32)
    for s in (0, 1):
        low = acts_all[s, :, :, :, hidden:].reshape(tokens, LANES).astype(F32)
        low = jnp.transpose(low)
        low = jnp.where(first, low[0:RANK], low[RANK:2 * RANK]).astype(BF16)
        rows = acts_all[s, :, :, :, 0:hidden].reshape(tokens, hidden)
        total += jnp.dot(low, rows, preferred_element_type=F32)
    up_mine[...] = ADAPTER_SCALE * total
    up_in = send(up_mine, up_theirs, to_dp)

    z_args = (n_z, z, core_sum, z_send, z_recv, z_next, {})
    for s in (0, 1):
        core_in[s].wait_recv()
        core_sum[s] = back[s, :, core] + core_recv[s]
        for d in (0, 1):
            reduce_step(*z_args, s, d, 0)
    for j in range(1, n_z // 2):
        for s in (0, 1):
            for d in (0, 1):
                reduce_step(*z_args, s, d, j)
    z_sum[1] = reduce_end(n_z, z, core_sum, z_recv, z_args[-1], 1)
    main_in = send(z_sum.at[1], dp_main, to_dp)
    z_sum[0] = reduce_end(n_z, z, core_sum, z_recv, z_args[-1], 0)
    dp_mine = z_sum.at[0, :, width:]
    ext_in = send(dp_mine, dp_ext, to_dp)
    main_in.wait_recv()
    ext_in.wait_recv()

    share = pl.ds(pl.multiple_of(fi * ROWS, ROWS), ROWS)
    own_ext = z_sum[0, :, width:] + dp_main[:, width:]
    low_own = own_ext.astype(BF16)
    low_other = (z_sum[1, :, width:] + dp_ext[...]).astype(BF16)
    normed_grad = (
        z_sum[0, :, 0:width]
        + dp_main[:, 0:width]
        + ADAPTER_SCALE * jnp.dot(low_own, down_ext[...], preferred_element_type=F32)
    )
    inv_here = cols[1, share]
    inner = jnp.sum(jnp.where(lane == 32, own_ext, 0.0), axis=1, keepdims=True) / model_width
    pull = inv_here * inv_here * inner
    for at, size in lanes:
        gathered[0, z, core, :, at:at + size] = (
            inv_here * gain[:, at:at + size] * normed_grad[:, at:at + size]
            - pull * steered[share, at:at + size]
        ).astype(BF16)
    gathered[0, z, core, :, width:width + LANES] = low_own
    gathered[0, z, core, :, width + LANES:] = low_other

    flying = {}
    mine_core = []
    held = gathered.at[0]

    def spread(origin):
        mine_core.append(send(held.at[origin, core], held.at[origin, core], to_core))

    spread(z)
    for j in range(n_z // 2):
        for d in (0, 1):
            count = hops(n_z, 0, d)
            if j < count:
                origin = lax.rem(z + (n_z - j if d == 0 else j), n_z)
                flying[d, j] = send(held.at[origin, core], held.at[origin, core], z_next[d])
        for d in (0, 1):
            count = hops(n_z, 0, d)
            if j < count:
                flying[d, j].wait_recv()
                spread(lax.rem(z + (n_z - j - 1 if d == 0 else j + 1), n_z))
    for copy in mine_core:
        copy.wait_recv()

    for at, size in lanes:
        piece = gathered[0, :, :, :, at:at + size].reshape(tokens, size)
        out_ref[:, at:at + size] = piece
        steer_mine[:, at:at + size] = jnp.sum(cols[0] * piece.astype(F32), axis=0, keepdims=True)
    steer_in = send(steer_mine, steer_theirs, to_dp)
    down = []
    for s in (0, 1):
        low = gathered[0, :, :, :, width + s * LANES:width + (s + 1) * LANES]
        low = jnp.transpose(low.reshape(tokens, LANES).astype(F32))[0:2 * RANK].astype(BF16)
        down.append(jnp.dot(low, normed[s], preferred_element_type=F32))
    down_grad_ref[...] = ADAPTER_SCALE * (down[0] + down[1])
    up_in.wait_recv()
    up_grad_ref[dp] = up_mine[...]
    up_grad_ref[1 - dp] = up_theirs[...]
    steer_in.wait_recv()
    steer_grad_ref[...] = steer_mine[...] + steer_theirs[...]
    for copy in started:
        copy.wait_send()


def solution(mesh):
    n_hid, n_ffn = mesh.shape["hid"], mesh.shape["ffn"]
    n_y, n_z = n_hid // 2, n_ffn // 2

    def local(stream, steering, strength, gain, weights, down, up, cotangent):
        tokens, width = stream.shape
        hidden = weights.shape[2]
        vmem = pl.BlockSpec(memory_space=pltpu.VMEM)
        ext = hidden + LANES
        y_hop = (2, 2, n_y // 2, 2 * ROWS, ext)
        z_hop = (2, 2, n_z // 2, ROWS, width + LANES)
        scratch = [
            ((width, hidden), BF16),
            ((tokens, width), BF16),
            ((n_hid, 8, tokens), F32),
            ((n_hid, 8, tokens), F32),
            ((8, tokens), F32),
            ((8, tokens), F32),
            ((tokens, width), F32),
            ((2, tokens, LANES), F32),
            ((2, tokens, width), BF16),
            ((2, n_y, 2 * ROWS, ext), F32),
            (y_hop, BF16),
            (y_hop, BF16),
            ((2, 2, ROWS, ext), F32),
            ((2, 2, ROWS, ext), BF16),
            ((3, ROWS, ext), BF16),
            ((LANES, ext), BF16),
            ((LANES, width), BF16),
            ((2, n_y, 2, ROWS, ext), BF16),
            ((ROWS, ext), BF16),
            ((2, n_z, 2, ROWS, width + LANES), F32),
            ((2, n_z, ROWS, width + LANES), F32),
            ((2, n_z, ROWS, width + LANES), F32),
            (z_hop, BF16),
            (z_hop, BF16),
            ((2, ROWS, width + LANES), F32),
            ((ROWS, width + LANES), F32),
            ((ROWS, LANES), F32),
            ((1, n_z, 2, ROWS, width + 2 * LANES), BF16),
            ((RANK, hidden), F32),
            ((RANK, hidden), F32),
            ((1, width), F32),
            ((1, width), F32),
        ]
        model_width = width * n_hid
        residual, steer_grad, down_grad, up_grad = pl.pallas_call(
            functools.partial(kernel, model_width, n_hid, n_ffn),
            out_shape=(
                jax.ShapeDtypeStruct((tokens, width), BF16),
                jax.ShapeDtypeStruct((1, width), F32),
                jax.ShapeDtypeStruct((2 * RANK, width), F32),
                jax.ShapeDtypeStruct((2, RANK, hidden), F32),
            ),
            in_specs=[vmem] * 4 + [pl.BlockSpec(memory_space=pl.ANY)] + [vmem] * 3,
            out_specs=(vmem,) * 4,
            scratch_shapes=[pltpu.VMEM(shape, dtype) for shape, dtype in scratch]
            + [
                pltpu.SemaphoreType.DMA((N_SEMS,)),
                pltpu.SemaphoreType.DMA((N_SEMS,)),
                pltpu.SemaphoreType.DMA,
            ],
            compiler_params=pltpu.CompilerParams(
                collective_id=0, has_side_effects=True, vmem_limit_bytes=60 * 1024 * 1024
            ),
            cost_estimate=pl.CostEstimate(
                flops=8 * tokens * width * hidden, bytes_accessed=2 * width * hidden, transcendentals=0
            ),
        )(
            stream,
            steering.reshape(1, width),
            strength.reshape(1, tokens),
            gain.reshape(1, width),
            weights.reshape(width, hidden),
            jnp.transpose(down, (0, 2, 1)).reshape(2 * RANK, width),
            up.reshape(2 * RANK, hidden),
            cotangent,
        )
        return (
            residual,
            steer_grad.reshape(width),
            jnp.transpose(down_grad.reshape(2, RANK, width), (0, 2, 1)),
            up_grad,
        )

    in_specs = (
        P("dp", "hid"),
        P("hid"),
        P("dp"),
        P("hid"),
        P("dp", "hid", "ffn"),
        P(None, "hid", None),
        P(None, None, "ffn"),
        P(("dp", "hid"), "ffn"),
    )
    out_specs = (P("dp", "hid"), P("hid"), P(None, "hid", None), P(None, None, "ffn"))
    return jax.shard_map(local, mesh=mesh, in_specs=in_specs, out_specs=out_specs, check_vma=False)
```

time: 485 us -> 133 us (0.27)
  blocking collectives: 238 us -> 0 us
  waiting for transfers between devices: 202 us -> 0 us
  Pallas kernels: 0 us -> 125 us
  matrix products: 20.7 us -> 0 us
  between operations: 14.6 us -> 0.64 us
    psum x6 -> x0, blocking collectives: 185 us -> none  [the longest x1 50.2 us: local(): preactivation_values, adapter_sum = lax.psum((full_acts, down_piece), 'hid')]
    pallas_call x0 -> x1, Pallas kernels: none -> 125 us  [local(): pl.pallas_call(functools.partial(kernel, model_width, n_hid, n_ffn), out_...]
    psum x2 -> x0, waiting for transfers between devices: 93.8 us -> none  [the longest x1 82.8 us: local(): preactivation_values, adapter_sum = lax.psum((full_acts, down_piece), 'hid')]
    reduce_scatter x1 -> x0, waiting for transfers between devices: 60.2 us -> none  [local(): lax.psum_scatter(jnp.einsum('tkf,kdf->td', activation_gradient, weights,...]
    all_gather x1 -> x0, blocking collectives: 53.1 us -> none  [local(): incoming_gradient = lax.all_gather(cotangent, 'hid', axis=0, tiled=True)]
    all_gather x2 -> x0, waiting for transfers between devices: 47.7 us -> none  [the longest x1 47.6 us: local(): weights = lax.all_gather(frozen_weights, 'dp', axis=0, tiled=True)]
    dot_general x7 -> x0, matrix products: 20.5 us -> none  [the longest x1 6.7 us: local(): jnp.einsum('td,kdf->tkf', normalized_input, weights, preferred_element_ty...]
  transfers between devices with their start and end apart: 5 -> 0, of which waited for: 4 -> 0; matrix products, arithmetic and copies ran while one was open for 2% -> 0% of each run, Pallas kernels for 0% -> 0%
where the time goes in v1:
time: 133 us; the launch traced here: 132 us
  Pallas kernels  125 us (94%)
  local copies, waits for them, and re-layouts  6.34 us (5%)
    pallas_call x1, Pallas kernels, local(): pl.pallas_call(functools.partial(kernel, model_width, n_hid, n_ffn), out_...  125 us
    unnamed x4, local copies, waits for them, and re-layouts  6.34 us

profile of v1, /device:TPU:1, one launch (start us, length us, event | category | flops | bytes accessed | tf_op | source)
XLA Modules:
  0.0 132.3 jit_solution(1531591514864023615)
XLA Ops:
  0.6 125.4 %shard_map.111 = (bf16[256,1024]{1,0:T(8,128)(2,1)}, f32[1,1024]{1,0:T(1,128)}, f32[32,1024]{1,0:T(8,128)}, f32[2,16,1664]{2,1,0:T(8,128)}) custom-call(bf16[256,1024]{1,0:T(8,128)(2,1)} %x_ref.1, f32[1,1024]{1,0:T(1,128)} %bitcast.17, f32[1,256]{1,0:T(1,128)} %bitcast.19, f32[1,1024]{1,0:T(1,128)} %bitcast.18, bf16[1024,1664]{1,0:T(8,128)(2,1)} %bitcast.14, ...), custom_call_target="tpu_custom_call" | custom-call | flops 3489660928 | bytes 3407872 | tf_op jit(solution)/shard_map/pallas_call | solution.py:425
  126.0 1.9 %copy.16 = bf16[256,1024]{1,0:T(8,128)(2,1)} copy(bf16[256,1024]{1,0:T(8,128)(2,1)} %get-tuple-element.16) | data formatting | bytes 1048576
  127.9 1.3 copy.17
  129.1 1.6 %copy.18 = f32[2,1024,16]{1,2,0:T(8,128)} copy(f32[2,1024,16]{1,2,0:T(8,128)} %bitcast.12) | data formatting | bytes 262144
  130.7 1.6 %copy.19 = f32[2,16,1664]{2,1,0:T(8,128)} copy(f32[2,16,1664]{2,1,0:T(8,128)} %get-tuple-element.19) | data formatting | bytes 425984

commit v2 on v1

v2 whole, which is shorter than its diff:
```python
import functools

import jax
import jax.numpy as jnp
from jax import lax
from jax.experimental import pallas as pl
from jax.experimental.pallas import tpu as pltpu
from jax.sharding import PartitionSpec as P

ADAPTER_SCALE = 0.5
RANK = 16
ROWS = 16
LANES = 128
MESH = pl.DeviceIdType.MESH
F32 = jnp.float32
BF16 = jnp.bfloat16
NT = (((1,), (1,)), ((), ()))
N_SEMS = 192


def tiles(total, size):
    return [(at, min(size, total - at)) for at in range(0, total, size)]


def row_to_columns(row):
    return jnp.transpose(jnp.broadcast_to(row, (LANES, row.shape[1])))


def columns_to_row(partial):
    return jnp.sum(jnp.transpose(partial), axis=0, keepdims=True)


def kernel(
    model_width, n_hid, n_ffn,
    x_ref, steer_ref, strength_ref, gain_ref, w_hbm, down_ref, up_ref, cot_ref,
    out_ref, steer_grad_ref, down_grad_ref, up_grad_ref,
    w_buf, x_other, stat_a, stat_b, ratio_mine, ratio_theirs, steered, cols, normed, partial, y_send, y_recv,
    y_block, x_recv, up_ext, down_ext, acts_all, acts_other, back, core_recv,
    z_send, z_recv, own_sum, gathered, low_mine, low_theirs, up_mine, up_theirs, steer_mine, steer_theirs,
    send_sem, recv_sem, z_send_sem, z_recv_sem, g_send_sem, g_recv_sem, local_sem,
):
    tokens, width = x_ref.shape
    hidden = w_hbm.shape[1]
    n_y, n_z = n_hid // 2, n_ffn // 2
    dp, fi, hi = lax.axis_index("dp"), lax.axis_index("ffn"), lax.axis_index("hid")
    y, xl, z, core = hi // 2, hi % 2, fi // 2, fi % 2
    first = dp == 0

    to_dp = {"dp": 1 - dp}
    to_xl = {"hid": hi + 1 - 2 * xl}
    to_diag = {"dp": 1 - dp, "hid": hi + 1 - 2 * xl}
    to_core = {"ffn": fi + 1 - 2 * core}
    y_next = ({"hid": lax.rem(hi + 2, n_hid)}, {"hid": lax.rem(hi + n_hid - 2, n_hid)})

    w_copy = pltpu.make_async_copy(w_hbm, w_buf, local_sem)
    w_copy.start()

    peers = [{"hid": lax.rem(hi + i, n_hid)} for i in range(1, n_hid)]
    peers += [{"dp": 1 - dp, "hid": lax.rem(hi + i, n_hid)} for i in range(n_hid)]
    for i in range(1, n_z):
        peers += [{"ffn": lax.rem(z + i, n_z) * 2 + core}]
        peers += [{"dp": 1 - dp, "ffn": lax.rem(z + i, n_z) * 2 + core}]
    peers += [to_core]
    barrier = pltpu.get_barrier_semaphore()
    for peer in peers:
        pl.semaphore_signal(barrier, inc=1, device_id=peer, device_id_type=MESH)
    pl.semaphore_wait(barrier, len(peers))

    started = []

    def send(src, dst, device):
        i = len(started)
        copy = pltpu.make_async_remote_copy(
            src_ref=src, dst_ref=dst, send_sem=send_sem.at[i], recv_sem=recv_sem.at[i],
            device_id=device, device_id_type=MESH,
        )
        copy.start()
        started.append(copy)
        return copy

    half = tokens // 2
    mine = pl.ds(pl.multiple_of(core * half, half), half)

    lanes = tiles(width, LANES)
    steer = steer_ref[...]
    gain = gain_ref[...]
    sub = lax.broadcasted_iota(jnp.int32, (4, tokens), 0)

    def share_stats(slots, value, batches):
        slots[0, hi] = value
        copies = []
        for i in range(n_hid):
            there = {"dp": 1 - dp, "hid": lax.rem(hi + i, n_hid)}
            if i:
                copies.append(send(slots.at[0, hi], slots.at[0, hi], {"hid": lax.rem(hi + i, n_hid)}))
            if batches == 2:
                copies.append(send(slots.at[0, hi], slots.at[1, hi], there))
        return copies

    def total_stats(slots, which):
        total = slots[which, 0]
        for i in range(1, n_hid):
            total = total + slots[which, i]
        return total

    squares = jnp.zeros((tokens, LANES), F32)
    crosses = jnp.zeros((tokens, LANES), F32)
    for at, size in lanes:
        piece = x_ref[:, at:at + size].astype(F32)
        squares += piece * piece
        crosses += piece * steer[:, at:at + size]
    steer_power = jnp.sum(steer * steer, axis=1, keepdims=True)
    rows = (columns_to_row(squares), steer_power, columns_to_row(crosses), strength_ref[...])
    packed = jnp.broadcast_to(rows[0], (4, tokens))
    for i in (1, 2, 3):
        packed = jnp.where(sub == i, jnp.broadcast_to(rows[i], (4, tokens)), packed)
    stat_in = share_stats(stat_a, packed, 2)
    stream_in = send(x_ref.at[mine], x_other.at[mine], to_dp)
    for copy in stat_in:
        copy.wait_recv()

    def rescale(which):
        total = total_stats(stat_a, which)
        power, steer_total, cross = total[0:1], total[1:2], total[2:3]
        scale = stat_a[which, 0, 3:4] * jnp.sqrt(
            (power / model_width + 1e-06) / (steer_total / model_width + 1e-06)
        )
        steered_power = power + scale * (2.0 * cross + scale * steer_total)
        steered_power = jnp.maximum(steered_power, 1e-07 * power)
        return scale, lax.rsqrt(steered_power / model_width + 1e-05)

    scale, inv_first = rescale(0)
    scale_other, inv_first_other = rescale(1)
    scale_cols = row_to_columns(scale)
    inv_cols = row_to_columns(inv_first)
    cols[0] = scale_cols
    squares = jnp.zeros((tokens, LANES), F32)
    for at, size in lanes:
        piece = x_ref[:, at:at + size].astype(F32) + scale_cols * steer[:, at:at + size]
        steered[:, at:at + size] = piece
        squares += piece * piece
        normed[0, :, at:at + size] = (piece * inv_cols * gain[:, at:at + size]).astype(BF16)

    up_ext[...] = jnp.zeros(up_ext.shape, BF16)
    up_ext[0:2 * RANK, 0:hidden] = up_ref[...]
    row = lax.broadcasted_iota(jnp.int32, (LANES, LANES), 0)
    col = lax.broadcasted_iota(jnp.int32, (LANES, LANES), 1)
    up_ext[:, hidden:] = jnp.where((row == 32) & ((col == 32) | (col == 33)), 1.0, 0.0).astype(BF16)
    down_ext[...] = jnp.zeros(down_ext.shape, BF16)
    down_ext[0:2 * RANK, :] = down_ref[...]

    w_copy.wait()

    def forward(which):
        rows = normed[which]
        for at, size in tiles(hidden, 256):
            block = jnp.dot(rows, w_buf[:, at:at + size], preferred_element_type=F32)
            partial[which, :, :, :, at:at + size] = block.reshape(n_y, 2, ROWS, size)
        block = lax.dot_general(rows, down_ext[...], NT, preferred_element_type=F32)
        partial[which, :, :, :, hidden:] = block.reshape(n_y, 2, ROWS, LANES)

    def hops(n, b, d):
        return n // 2 if (b + d) % 2 == 0 else n // 2 - 1

    sums_of = ((0, 1 - xl), (1, xl), (1, 1 - xl), (0, xl))

    def reduce_step(n, me, terms, sends, recvs, nexts, flying, b, d, j):
        count = hops(n, b, d)
        if j >= count:
            return
        k = count - j
        owner = lax.rem(me + (k if d == 0 else n - k), n)
        batch, low = sums_of[b]
        value = terms[batch, owner, low]
        if j:
            flying[b, d, j - 1].wait_recv()
            value = value + recvs[b, d, j - 1].astype(F32)
        sends[b, d, j] = value.astype(BF16)
        flying[b, d, j] = send(sends.at[b, d, j], recvs.at[b, d, j], nexts[d])

    def reduce_end(n, me, terms, sends, recvs, nexts, flying, b):
        batch, low = sums_of[b]
        value = terms[batch, me, low]
        for d in (0, 1):
            count = hops(n, b, d)
            if count:
                flying[b, d, count - 1].wait_recv()
                value = value + recvs[b, d, count - 1].astype(F32)
        return value

    grads_of = ((0, xl), (0, 1 - xl), (1, xl), (1, 1 - xl))

    def gather_step(n, me, held, nexts, flying, b, d, j):
        if j >= hops(n, b, d):
            return
        if j:
            flying[b, d, j - 1].wait_recv()
        origin = lax.rem(me + (n - j if d == 0 else j), n)
        batch, low = grads_of[b]
        block = held.at[batch, origin, low]
        flying[b, d, j] = send(block, block, nexts[d])

    y_args = (n_y, y, partial, y_send, y_recv, y_next, {})
    forward(0)
    for b in (0, 3):
        for d in (0, 1):
            reduce_step(*y_args, b, d, 0)
    exact_in = share_stats(stat_b, jnp.broadcast_to(columns_to_row(squares), (4, tokens)), 1)

    stream_in.wait_recv()
    stream_core = send(x_other.at[mine], x_other.at[mine], to_core)
    stream_core.wait_recv()
    scale_other = row_to_columns(scale_other)
    inv_other = row_to_columns(inv_first_other)
    for at, size in lanes:
        piece = x_other[:, at:at + size].astype(F32) + scale_other * steer[:, at:at + size]
        normed[1, :, at:at + size] = (piece * inv_other * gain[:, at:at + size]).astype(BF16)
    forward(1)
    for b in (1, 2):
        for d in (0, 1):
            reduce_step(*y_args, b, d, 0)
    for j in range(1, n_y // 2):
        for b in range(4):
            for d in (0, 1):
                reduce_step(*y_args, b, d, j)
    x_in = []
    for b, there in enumerate((to_xl, to_dp, to_diag)):
        y_block[b] = reduce_end(*y_args, b).astype(BF16)
        x_in.append(send(y_block.at[b], x_recv.at[b], there))
    own_block = reduce_end(*y_args, 3)

    for copy in exact_in:
        copy.wait_recv()
    inv = lax.rsqrt(total_stats(stat_b, 0)[0:1] / model_width + 1e-05)
    ratio = inv / inv_first
    cols[1] = row_to_columns(inv)
    cols[2] = row_to_columns(ratio)
    ratio_mine[...] = jnp.broadcast_to(ratio, ratio_mine.shape)
    for copy in x_in:
        copy.wait_recv()
    ratio_in = send(ratio_mine, ratio_theirs, to_dp)

    fix = cols[2, pl.ds(pl.multiple_of(hi * ROWS, ROWS), ROWS)][:, 0:1]
    acts_same = (own_block + x_recv[0].astype(F32)) * fix
    acts_cross = (x_recv[1].astype(F32) + x_recv[2].astype(F32)) * fix
    gate = jnp.where(first, acts_same, acts_cross)
    up = jnp.where(first, acts_cross, acts_same)
    lane = lax.broadcasted_iota(jnp.int32, (ROWS, LANES), 1)
    low_gate = jnp.where(lane < RANK, gate[:, hidden:], 0.0).astype(BF16)
    low_up = jnp.where((lane >= RANK) & (lane < 2 * RANK), up[:, hidden:], 0.0).astype(BF16)
    factors = up_ext[:, 0:hidden]
    gate = gate[:, 0:hidden] + ADAPTER_SCALE * jnp.dot(low_gate, factors, preferred_element_type=F32)
    up = up[:, 0:hidden] + ADAPTER_SCALE * jnp.dot(low_up, factors, preferred_element_type=F32)
    sigma = 1.0 / (1.0 + jnp.exp(-gate))
    flow = cot_ref[...].astype(F32)
    gate_grad = (flow * up * sigma * (1.0 + gate * (1.0 - sigma))).astype(BF16)
    upper_grad = (flow * gate * sigma).astype(BF16)

    def ext_columns(low, grad, acts):
        inner = jnp.sum(grad.astype(F32) * acts, axis=1, keepdims=True)
        high = inner.astype(BF16).astype(F32)
        rest = jnp.where(lane == 32, high, jnp.where(lane == 33, inner - high, 0.0))
        return low.astype(F32) + rest

    gate_ext = ext_columns(low_gate, gate_grad, gate)
    upper_ext = ext_columns(low_up, upper_grad, up)
    gate_grad, upper_grad = gate_grad.astype(F32), upper_grad.astype(F32)
    acts_all[0, y, xl, :, 0:hidden] = jnp.where(first, gate_grad, upper_grad).astype(BF16)
    acts_all[0, y, xl, :, hidden:] = jnp.where(first, gate_ext, upper_ext).astype(BF16)
    acts_other[:, 0:hidden] = jnp.where(first, upper_grad, gate_grad).astype(BF16)
    acts_other[:, hidden:] = jnp.where(first, upper_ext, gate_ext).astype(BF16)

    x_out = [
        send(acts_all.at[0, y, xl], acts_all.at[0, y, xl], to_xl),
        send(acts_other, acts_all.at[1, y, xl], to_dp),
        send(acts_other, acts_all.at[1, y, xl], to_diag),
    ]
    g_args = (n_y, y, acts_all, y_next, {})
    for b in range(4):
        if b:
            x_out[b - 1].wait_recv()
        for d in (0, 1):
            gather_step(*g_args, b, d, 0)

    lane64 = lax.broadcasted_iota(jnp.int32, (4 * ROWS, LANES), 1)
    keep = ((lane64 >= RANK * dp) & (lane64 < RANK * dp + RANK)) | (lane64 == 32)
    half_z = n_z // 2

    def backward(slots, origins):
        shape = (2, 2, ROWS)
        rows = [acts_all[s, o].reshape(2 * ROWS, hidden + LANES) for o in origins for s in (0, 1)]
        rows = jnp.concatenate(rows, axis=0)
        for at, size in tiles(width, 256):
            block = lax.dot_general(
                rows[:, 0:hidden], w_buf[at:at + size, :], NT, preferred_element_type=F32
            )
            for i, q in enumerate(slots):
                back[q, :, :, :, at:at + size] = block[i * 64:(i + 1) * 64].reshape(*shape, size)
        block = lax.dot_general(rows, up_ext[...], NT, preferred_element_type=F32)
        for i, q in enumerate(slots):
            piece = jnp.where(keep, block[i * 64:(i + 1) * 64], 0.0)
            back[q, :, :, :, width:] = piece.reshape(*shape, LANES)
        return [send(back.at[q, :, 1 - core], core_recv.at[q], to_core) for q in slots]

    def scatter(slots, origins, core_in):
        for q, origin, copy in zip(slots, origins, core_in):
            copy.wait_recv()
            value = back[q, :, core] + core_recv[q]
            z_send[q] = value.astype(BF16)
            owner = lax.rem(origin + half_z * core, n_z)
            there = pltpu.make_async_remote_copy(
                src_ref=z_send.at[q, 1], dst_ref=z_recv.at[1, z],
                send_sem=z_send_sem.at[1, q], recv_sem=z_recv_sem.at[1, z],
                device_id={"dp": 1 - dp, "ffn": owner * 2 + core}, device_id_type=MESH,
            )
            here = pltpu.make_async_remote_copy(
                src_ref=z_send.at[q, 0], dst_ref=z_recv.at[0, z],
                send_sem=z_send_sem.at[0, q], recv_sem=z_recv_sem.at[0, z],
                device_id={"ffn": owner * 2 + core}, device_id_type=MESH,
            )
            there.start()
            started.append(there)

            @pl.when(owner != z)
            def _():
                here.start()

            @pl.when(owner == z)
            def _():
                own_sum[...] = value[0]

            z_started.append((owner, here))

    z_started = []
    waiting = None
    for j in range(n_y // 2 + 1):
        if j == 0:
            slots, origins = [0], [y]
        elif j == n_y // 2:
            slots, origins = [n_y - 1], [lax.rem(y + j, n_y)]
        else:
            slots, origins = [2 * j - 1, 2 * j], [lax.rem(y + n_y - j, n_y), lax.rem(y + j, n_y)]
        if j:
            for b in range(4):
                for d in (0, 1):
                    if j < hops(n_y, b, d):
                        gather_step(*g_args, b, d, j)
                    elif j == hops(n_y, b, d):
                        g_args[-1][b, d, j - 1].wait_recv()
        core_in = backward(slots, origins)
        if waiting is not None:
            scatter(*waiting)
        waiting = (slots, origins, core_in)
    scatter(*waiting)

    total = jnp.zeros((RANK, hidden), F32)
    for s in (0, 1):
        low = acts_all[s, :, :, :, hidden:].reshape(tokens, LANES).astype(F32)
        low = jnp.transpose(low)
        low = jnp.where(first, low[0:RANK], low[RANK:2 * RANK]).astype(BF16)
        rows = acts_all[s, :, :, :, 0:hidden].reshape(tokens, hidden)
        total += jnp.dot(low, rows, preferred_element_type=F32)
    up_mine[...] = ADAPTER_SCALE * total
    up_in = send(up_mine, up_theirs, to_dp)

    def arrived(from_other, source):
        pltpu.make_async_remote_copy(
            src_ref=z_send.at[0, 0], dst_ref=z_recv.at[from_other, source],
            send_sem=z_send_sem.at[0, 0], recv_sem=z_recv_sem.at[from_other, source],
            device_id=to_dp, device_id_type=MESH,
        ).wait_recv()

    for i in range(1, n_z):
        arrived(0, lax.rem(z + i, n_z))
    for i in range(n_z):
        arrived(1, i)
    total = own_sum[...]
    for i in range(1, n_z):
        total = total + z_recv[0, lax.rem(z + i, n_z)].astype(F32)
    for i in range(n_z):
        total = total + z_recv[1, i].astype(F32)

    held = lax.rem(z + n_z - half_z * core, n_z)
    share = pl.ds(pl.multiple_of((held * 2 + core) * ROWS, ROWS), ROWS)
    own_ext = total[:, width:]
    low_own = own_ext.astype(BF16)
    normed_grad = total[:, 0:width] + ADAPTER_SCALE * jnp.dot(
        low_own, down_ext[...], preferred_element_type=F32
    )
    inv_here = cols[1, share]
    inner = jnp.sum(jnp.where(lane == 32, own_ext, 0.0), axis=1, keepdims=True) / model_width
    pull = inv_here * inv_here * inner
    for at, size in lanes:
        gathered[held, core, :, at:at + size] = (
            inv_here * gain[:, at:at + size] * normed_grad[:, at:at + size]
            - pull * steered[share, at:at + size]
        ).astype(BF16)
    gathered[held, core, :, width:] = low_own
    low_mine[...] = low_own

    def spread(source_z, i):
        block = lax.rem(source_z + n_z - half_z * core, n_z)
        target = lax.rem(z + i, n_z) * 2 + core
        return pltpu.make_async_remote_copy(
            src_ref=gathered.at[block, core], dst_ref=gathered.at[block, core],
            send_sem=g_send_sem.at[0, i], recv_sem=g_recv_sem.at[0, source_z],
            device_id={"ffn": target}, device_id_type=MESH,
        )

    def spread_low(source_z, i):
        block = lax.rem(source_z + n_z - half_z * core, n_z)
        target = lax.rem(z + i, n_z) * 2 + core
        return pltpu.make_async_remote_copy(
            src_ref=low_mine, dst_ref=low_theirs.at[core, block],
            send_sem=g_send_sem.at[1, i], recv_sem=g_recv_sem.at[1, source_z],
            device_id={"dp": 1 - dp, "ffn": target}, device_id_type=MESH,
        )

    order = [0] + [i for j in range(1, half_z + 1) for i in dict.fromkeys((j, n_z - j))]
    for i in order[1:]:
        copy = spread(z, i)
        copy.start()
        started.append(copy)
    for i in order:
        copy = spread_low(z, i)
        copy.start()
        started.append(copy)
    from_core = []
    for i in order:
        source = lax.rem(z + n_z - i, n_z)
        block = lax.rem(source + n_z - half_z * core, n_z)
        if i:
            spread(source, i).wait_recv()
        from_core.append(send(gathered.at[block, core], gathered.at[block, core], to_core))
    for i in order:
        spread_low(lax.rem(z + n_z - i, n_z), i).wait_recv()
    from_core.append(send(low_theirs.at[core], low_theirs.at[core], to_core))
    for copy in from_core:
        copy.wait_recv()

    for at, size in lanes:
        piece = gathered[:, :, :, at:at + size].reshape(tokens, size)
        out_ref[:, at:at + size] = piece
        steer_mine[:, at:at + size] = jnp.sum(cols[0] * piece.astype(F32), axis=0, keepdims=True)
    steer_in = send(steer_mine, steer_theirs, to_dp)
    lows = (
        gathered[:, :, :, width:].reshape(tokens, LANES),
        jnp.concatenate([low_theirs[c, o] for o in range(n_z) for c in (0, 1)], axis=0),
    )
    down = []
    ratio_in.wait_recv()
    ratios = (ratio, ratio_theirs[0:1])
    for s in (0, 1):
        low = jnp.transpose(lows[s].astype(F32))[0:2 * RANK] * ratios[s]
        down.append(jnp.dot(low.astype(BF16), normed[s], preferred_element_type=F32))
    down_grad_ref[...] = ADAPTER_SCALE * (down[0] + down[1])
    up_in.wait_recv()
    up_grad_ref[dp] = up_mine[...]
    up_grad_ref[1 - dp] = up_theirs[...]
    steer_in.wait_recv()
    steer_grad_ref[...] = steer_mine[...] + steer_theirs[...]
    for copy in started:
        copy.wait_send()
    for owner, copy in z_started:

        @pl.when(owner != z)
        def _(copy=copy):
            copy.wait_send()


def hand_over(*refs):
    n = len(refs) // 2
    for i in range(n):
        refs[n + i][...] = refs[i][...]


def solution(mesh):
    n_hid, n_ffn = mesh.shape["hid"], mesh.shape["ffn"]
    n_y, n_z = n_hid // 2, n_ffn // 2

    def local(stream, steering, strength, gain, weights, down, up, cotangent):
        tokens, width = stream.shape
        hidden = weights.shape[2]
        vmem = pl.BlockSpec(memory_space=pltpu.VMEM)
        ext = hidden + LANES
        y_hop = (4, 2, n_y // 2, ROWS, ext)
        scratch = [
            ((width, hidden), BF16),
            ((tokens, width), BF16),
            ((2, n_hid, 4, tokens), F32),
            ((1, n_hid, 4, tokens), F32),
            ((4, tokens), F32),
            ((4, tokens), F32),
            ((tokens, width), F32),
            ((3, tokens, LANES), F32),
            ((2, tokens, width), BF16),
            ((2, n_y, 2, ROWS, ext), F32),
            (y_hop, BF16),
            (y_hop, BF16),
            ((3, ROWS, ext), BF16),
            ((3, ROWS, ext), BF16),
            ((LANES, ext), BF16),
            ((LANES, width), BF16),
            ((2, n_y, 2, ROWS, ext), BF16),
            ((ROWS, ext), BF16),
            ((n_z, 2, 2, ROWS, width + LANES), F32),
            ((n_z, 2, ROWS, width + LANES), F32),
            ((n_z, 2, ROWS, width + LANES), BF16),
            ((2, n_z, ROWS, width + LANES), BF16),
            ((ROWS, width + LANES), F32),
            ((n_z, 2, ROWS, width + LANES), BF16),
            ((ROWS, LANES), BF16),
            ((2, n_z, ROWS, LANES), BF16),
            ((RANK, hidden), F32),
            ((RANK, hidden), F32),
            ((1, width), F32),
            ((1, width), F32),
        ]
        model_width = width * n_hid
        residual, steer_grad, down_grad, up_grad = pl.pallas_call(
            functools.partial(kernel, model_width, n_hid, n_ffn),
            out_shape=(
                jax.ShapeDtypeStruct((tokens, width), BF16),
                jax.ShapeDtypeStruct((1, width), F32),
                jax.ShapeDtypeStruct((2 * RANK, width), F32),
                jax.ShapeDtypeStruct((2, RANK, hidden), F32),
            ),
            in_specs=[vmem] * 4 + [pl.BlockSpec(memory_space=pl.ANY)] + [vmem] * 3,
            out_specs=(vmem,) * 4,
            scratch_shapes=[pltpu.VMEM(shape, dtype) for shape, dtype in scratch]
            + [
                pltpu.SemaphoreType.DMA((N_SEMS,)),
                pltpu.SemaphoreType.DMA((N_SEMS,)),
                pltpu.SemaphoreType.DMA((2, n_z)),
                pltpu.SemaphoreType.DMA((2, n_z)),
                pltpu.SemaphoreType.DMA((2, n_z)),
                pltpu.SemaphoreType.DMA((2, n_z)),
                pltpu.SemaphoreType.DMA,
            ],
            compiler_params=pltpu.CompilerParams(
                collective_id=0, has_side_effects=True, vmem_limit_bytes=60 * 1024 * 1024
            ),
            cost_estimate=pl.CostEstimate(
                flops=8 * tokens * width * hidden, bytes_accessed=2 * width * hidden, transcendentals=0
            ),
        )(
            stream,
            steering.reshape(1, width),
            strength.reshape(1, tokens),
            gain.reshape(1, width),
            weights.reshape(width, hidden),
            jnp.transpose(down, (0, 2, 1)).reshape(2 * RANK, width),
            up.reshape(2 * RANK, hidden),
            cotangent,
        )
        results = (residual, steer_grad, down_grad, up_grad)
        residual, steer_grad, down_grad, up_grad = pl.pallas_call(
            hand_over,
            out_shape=tuple(jax.ShapeDtypeStruct(r.shape, r.dtype) for r in results),
            in_specs=[vmem] * 4,
            out_specs=(vmem,) * 4,
        )(*results)
        return (
            residual,
            steer_grad.reshape(width),
            jnp.transpose(down_grad.reshape(2, RANK, width), (0, 2, 1)),
            up_grad,
        )

    in_specs = (
        P("dp", "hid"),
        P("hid"),
        P("dp"),
        P("hid"),
        P("dp", "hid", "ffn"),
        P(None, "hid", None),
        P(None, None, "ffn"),
        P(("dp", "hid"), "ffn"),
    )
    out_specs = (P("dp", "hid"), P("hid"), P(None, "hid", None), P(None, None, "ffn"))
    return jax.shard_map(local, mesh=mesh, in_specs=in_specs, out_specs=out_specs, check_vma=False)
```

time: 133 us -> 110 us (0.83)
  Pallas kernels: 125 us -> 109 us
  local copies, waits for them, and re-layouts: 6.34 us -> 0 us
    pallas_call x1, Pallas kernels: 125 us -> 107 us  [local(): pl.pallas_call(functools.partial(kernel, model_width, n_hid, n_ffn), out_...]
    unnamed x4 -> x0, local copies, waits for them, and re-layouts: 6.34 us -> none
    pallas_call x0 -> x1, Pallas kernels: none -> 2.07 us  [local(): pl.pallas_call(hand_over, out_shape=tuple((jax.ShapeDtypeStruct(r.shape,...]
where the time goes in v2:
time: 110 us
  Pallas kernels  109 us (99%)
    pallas_call x1, Pallas kernels, local(): pl.pallas_call(functools.partial(kernel, model_width, n_hid, n_ffn), out_...  107 us

profile of v2, /device:TPU:1, one launch (start us, length us, event | category | flops | bytes accessed | tf_op | source)
XLA Modules:
  0.0 109.8 jit_solution(12413976334666143082)
XLA Ops:
  0.6 107.1 %shard_map.111 = (bf16[256,1024]{1,0:T(8,128)(2,1)}, f32[1,1024]{1,0:T(1,128)}, f32[32,1024]{1,0:T(8,128)}, f32[2,16,1664]{2,1,0:T(8,128)}) custom-call(bf16[256,1024]{1,0:T(8,128)(2,1)} %x_ref.1, f32[1,1024]{1,0:T(1,128)} %bitcast.16, f32[1,256]{1,0:T(1,128)} %bitcast.19, f32[1,1024]{1,0:T(1,128)} %bitcast.17, bf16[1024,1664]{1,0:T(8,128)(2,1)} %bitcast.12, ...), custom_call_target="tpu_custom_call" | custom-call | flops 3489660928 | bytes 3407872 | tf_op jit(solution)/shard_map/pallas_call | solution.py:520
  107.7 2.1 %shard_map.112 = (bf16[256,1024]{1,0:T(8,128)(2,1)}, f32[1,1024]{1,0:T(1,128)}, f32[32,1024]{1,0:T(8,128)}, f32[2,16,1664]{2,1,0:T(8,128)}) custom-call(bf16[256,1024]{1,0:T(8,128)(2,1)} %get-tuple-element.12.refs_0_, f32[1,1024]{1,0:T(1,128)} %get-tuple-element.13.refs_1_, f32[32,1024]{1,0:T(8,128)} %get-tuple-element.14.refs_2_, ...), custom_call_target="tpu_custom_call" | custom-call | tf_op jit(solution)/shard_map/pallas_call | solution.py:557
